TPU v7x, 32 devices: a whole 2x2x4 slice. The times are simulated.
32 devices in a mesh: groups: 2 (over x), blk: 8 (over z, y), docs: 2 (over core).
Axes of the slice: x: 2, y: 2, z: 4, core: 2. Of those that a mesh axis runs over, the one named last changes fastest.
Arguments:
- queries: bfloat16 [128, 2048], P(('groups', 'blk')), parts along dimension 0, may hold values from -6 to 6
- whiten: bfloat16 [4096, 2048], P(('groups', 'blk', 'docs')), parts along dimension 0, may hold values from -1 to 2
- documents: float32 [32768, 2048], P(('groups', 'blk', 'docs')), parts along dimension 0, may hold values from -600 to 600
Outputs:
- standardized: float32 [128, 16384], P('groups', ('blk', 'docs')), parts along dimension 0
There are 2 independent parts, one for each index of `groups`. A program takes and returns all parts, laid end to end along the dimension named above; each array names one. Nothing has to cross between parts.
All inputs are finite; a program needn't handle non-finite values.
Results may differ from a plain program's by a relative error of at most 0.0003.
Values may be sent and summed in bfloat16 or wider, within the bound.
A program may use at most 64 MiB of HBM per device.

v0:
```python
import jax
import jax.numpy as jnp
from jax import lax
from jax.sharding import PartitionSpec as P


def from_behind(value, axis, by):
    length = lax.axis_size(axis)
    return lax.ppermute(value, axis, [(i, (i + by) % length) for i in range(length)])


def block_scores(block, documents):
    return lax.dot_general(
        block,
        documents,
        (((1,), (1,)), ((), ())),
        precision=lax.Precision.HIGHEST,
        preferred_element_type=jnp.float32,
    )


def per_device(queries, whiten, documents):
    q_rows = queries.shape[0]
    n_blk = lax.axis_size("blk")
    n_docs = lax.axis_size("docs")
    here = lax.axis_index("blk")
    core = lax.axis_index("docs")
    span = whiten.shape[0]
    owner_index = here * n_docs + core
    all_queries = lax.all_gather(queries, "blk", axis=0, tiled=True)
    query_cols = lax.dynamic_slice_in_dim(all_queries, owner_index * span, span, 1)
    own_share = lax.psum_scatter(
        jnp.dot(query_cols, whiten, preferred_element_type=jnp.float32),
        ("blk", "docs"),
        scatter_dimension=0,
        tiled=True,
    )
    whitened = lax.all_gather(own_share, "docs", axis=0, tiled=True)

    def place(scores, block, owner):
        return lax.dynamic_update_slice_in_dim(
            scores, block_scores(block, documents), owner * q_rows, 0
        )

    scores = jnp.zeros((q_rows * n_blk, documents.shape[0]), jnp.float32)
    scores = place(scores, whitened, here)

    def step_one(turn, carry):
        held, moving = carry
        moving = from_behind(moving, "blk", 1)
        held = place(held, moving, (here - turn) % n_blk)
        return (held, moving)

    scores, moving = lax.fori_loop(1, n_blk, step_one, (scores, whitened))
    count = jnp.float32(documents.shape[0] * n_blk * n_docs)
    total = lax.psum(jnp.sum(scores, axis=1), ("blk", "docs"))
    mean = total / count
    centered = scores - mean[:, None]
    spread = lax.psum(jnp.sum(centered * centered, axis=1), ("blk", "docs"))
    variance = spread / count
    return centered * lax.rsqrt(variance + 1e-05)[:, None]


def solution(mesh):
    placed = (
        P(("groups", "blk"), None),
        P(("groups", "blk", "docs"), None),
        P(("groups", "blk", "docs"), None),
    )
    return jax.shard_map(
        per_device,
        mesh=mesh,
        in_specs=placed,
        out_specs=P("groups", ("blk", "docs")),
        check_vma=False,
    )
```

profile of v0, /device:TPU:0, one launch (start us, length us, event | category | flops | bytes accessed | tf_op | source)
XLA Modules:
  0.0 324.0 jit_solution(7387192498760915884)
XLA Ops:
  6.5 32.9 %all_gather.6 = bf16[64,2048]{1,0:T(8,128)(2,1)S(1)} all-gather(bf16[8,2048]{1,0:T(8,128)(2,1)} %param.5), channel_id=1, replica_groups=mesh['groups'=2,'blk'=8,'docs'=2] {'blk'}, dimensions={0}, use_global_device_ids=true | all-gather | bytes 294912 | tf_op jit(solution)/shard_map/all_gather | solution.py:30
  39.4 1.0 fusion
  40.5 1.2 dynamic-slice
  42.3 89.4 %all-reduce.3.cloned.1.call-done = f32[64,2048]{1,0:T(8,128)} async-done(((f32[64,2048]{1,0:T(8,128)}), f32[64,2048]{1,0:T(8,128)}) %all-reduce.3.cloned.1.call-update) | async-done | bytes 524304
  131.7 0.8 dynamic-slice_bitcast_fusion
  132.6 2.0 all-gather
  134.6 9.2 %convolution_dynamic-update-slice_fusion.1 = f32[64,1024]{1,0:T(8,128)S(1)} fusion(f32[64,1024]{1,0:T(8,128)S(1)} %broadcast_in_dim.2, s32[]{:T(128)S(6)} %select_n.37, f32[8,2048]{1,0:T(8,128)S(1)} %reshape.3, f32[1024,2048]{1,0:T(8,128)} %param.7), kind=kOutput, calls=%fused_computation.1 | convolution fusion | flops 201326592 | bytes 8486916 | tf_op jit(solution)/shard_map/dot_general | solution.py:13
  143.8 113.2 %while.17 = (s32[]{:T(128)}, f32[64,1024]{1,0:T(8,128)S(1)}, f32[8,2048]{1,0:T(8,128)S(1)}, f32[1024,2048]{1,0:T(8,128)}, s32[]{:T(128)}, /*index=5*/s32[]{:T(128)}, s32[]{:T(128)}, s32[]{:T(128)}, s32[]{:T(128)}, s32[]{:T(128)}) while((s32[]{:T(128)}, f32[64,1024]{1,0:T(8,128)S(1)}, f32[8,2048]{1,0:T(8,128)S(1)}, f32[1024,2048]{1,0:T(8,128)}, ...), condition=%wide.region_2.3_spmd, body=%wide.region_1.2_spmd.sunk | while | flops 201326608 | bytes 8880440 | solution.py:54
  144.4 6.5 %collective-permute-done = f32[8,2048]{1,0:T(8,128)S(1)} collective-permute-done((f32[8,2048]{1,0:T(8,128)S(1)}, f32[8,2048]{1,0:T(8,128)S(1)}, u32[]{:S(2)}, u32[]{:S(2)}) %collective-permute-start) | collective-permute-done | bytes 65568 | tf_op jit(solution)/shard_map/while/body/eval_jaxpr/ppermute | solution.py:9
  150.8 9.2 %convolution_dynamic-update-slice_fusion.3 = f32[64,1024]{1,0:T(8,128)S(1)} fusion(f32[64,1024]{1,0:T(8,128)S(1)} %get-tuple-element.191, s32[]{:T(128)S(6)} %select_n.41, f32[8,2048]{1,0:T(8,128)S(1)} %collective-permute-done, f32[1024,2048]{1,0:T(8,128)} %get-tuple-element.203), kind=kOutput, calls=%fused_computation.clone.1 | convolution fusion | flops 201326592 | bytes 8486916 | tf_op jit(solution)/shard_map/while/body/eval_jaxpr/dot_general | solution.py:13
  160.0 6.9 %collective-permute-done = f32[8,2048]{1,0:T(8,128)S(1)} collective-permute-done((f32[8,2048]{1,0:T(8,128)S(1)}, f32[8,2048]{1,0:T(8,128)S(1)}, u32[]{:S(2)}, u32[]{:S(2)}) %collective-permute-start) | collective-permute-done | bytes 65568 | tf_op jit(solution)/shard_map/while/body/eval_jaxpr/ppermute | solution.py:9
  167.0 9.2 %convolution_dynamic-update-slice_fusion.3 = f32[64,1024]{1,0:T(8,128)S(1)} fusion(f32[64,1024]{1,0:T(8,128)S(1)} %get-tuple-element.191, s32[]{:T(128)S(6)} %select_n.41, f32[8,2048]{1,0:T(8,128)S(1)} %collective-permute-done, f32[1024,2048]{1,0:T(8,128)} %get-tuple-element.203), kind=kOutput, calls=%fused_computation.clone.1 | convolution fusion | flops 201326592 | bytes 8486916 | tf_op jit(solution)/shard_map/while/body/eval_jaxpr/dot_general | solution.py:13
  176.2 6.9 %collective-permute-done = f32[8,2048]{1,0:T(8,128)S(1)} collective-permute-done((f32[8,2048]{1,0:T(8,128)S(1)}, f32[8,2048]{1,0:T(8,128)S(1)}, u32[]{:S(2)}, u32[]{:S(2)}) %collective-permute-start) | collective-permute-done | bytes 65568 | tf_op jit(solution)/shard_map/while/body/eval_jaxpr/ppermute | solution.py:9
  183.2 9.2 %convolution_dynamic-update-slice_fusion.3 = f32[64,1024]{1,0:T(8,128)S(1)} fusion(f32[64,1024]{1,0:T(8,128)S(1)} %get-tuple-element.191, s32[]{:T(128)S(6)} %select_n.41, f32[8,2048]{1,0:T(8,128)S(1)} %collective-permute-done, f32[1024,2048]{1,0:T(8,128)} %get-tuple-element.203), kind=kOutput, calls=%fused_computation.clone.1 | convolution fusion | flops 201326592 | bytes 8486916 | tf_op jit(solution)/shard_map/while/body/eval_jaxpr/dot_general | solution.py:13
  192.4 6.9 %collective-permute-done = f32[8,2048]{1,0:T(8,128)S(1)} collective-permute-done((f32[8,2048]{1,0:T(8,128)S(1)}, f32[8,2048]{1,0:T(8,128)S(1)}, u32[]{:S(2)}, u32[]{:S(2)}) %collective-permute-start) | collective-permute-done | bytes 65568 | tf_op jit(solution)/shard_map/while/body/eval_jaxpr/ppermute | solution.py:9
  199.3 9.2 %convolution_dynamic-update-slice_fusion.3 = f32[64,1024]{1,0:T(8,128)S(1)} fusion(f32[64,1024]{1,0:T(8,128)S(1)} %get-tuple-element.191, s32[]{:T(128)S(6)} %select_n.41, f32[8,2048]{1,0:T(8,128)S(1)} %collective-permute-done, f32[1024,2048]{1,0:T(8,128)} %get-tuple-element.203), kind=kOutput, calls=%fused_computation.clone.1 | convolution fusion | flops 201326592 | bytes 8486916 | tf_op jit(solution)/shard_map/while/body/eval_jaxpr/dot_general | solution.py:13
  208.5 6.9 %collective-permute-done = f32[8,2048]{1,0:T(8,128)S(1)} collective-permute-done((f32[8,2048]{1,0:T(8,128)S(1)}, f32[8,2048]{1,0:T(8,128)S(1)}, u32[]{:S(2)}, u32[]{:S(2)}) %collective-permute-start) | collective-permute-done | bytes 65568 | tf_op jit(solution)/shard_map/while/body/eval_jaxpr/ppermute | solution.py:9
  215.5 9.2 %convolution_dynamic-update-slice_fusion.3 = f32[64,1024]{1,0:T(8,128)S(1)} fusion(f32[64,1024]{1,0:T(8,128)S(1)} %get-tuple-element.191, s32[]{:T(128)S(6)} %select_n.41, f32[8,2048]{1,0:T(8,128)S(1)} %collective-permute-done, f32[1024,2048]{1,0:T(8,128)} %get-tuple-element.203), kind=kOutput, calls=%fused_computation.clone.1 | convolution fusion | flops 201326592 | bytes 8486916 | tf_op jit(solution)/shard_map/while/body/eval_jaxpr/dot_general | solution.py:13
  224.7 6.9 %collective-permute-done = f32[8,2048]{1,0:T(8,128)S(1)} collective-permute-done((f32[8,2048]{1,0:T(8,128)S(1)}, f32[8,2048]{1,0:T(8,128)S(1)}, u32[]{:S(2)}, u32[]{:S(2)}) %collective-permute-start) | collective-permute-done | bytes 65568 | tf_op jit(solution)/shard_map/while/body/eval_jaxpr/ppermute | solution.py:9
  231.6 9.2 %convolution_dynamic-update-slice_fusion.3 = f32[64,1024]{1,0:T(8,128)S(1)} fusion(f32[64,1024]{1,0:T(8,128)S(1)} %get-tuple-element.191, s32[]{:T(128)S(6)} %select_n.41, f32[8,2048]{1,0:T(8,128)S(1)} %collective-permute-done, f32[1024,2048]{1,0:T(8,128)} %get-tuple-element.203), kind=kOutput, calls=%fused_computation.clone.1 | convolution fusion | flops 201326592 | bytes 8486916 | tf_op jit(solution)/shard_map/while/body/eval_jaxpr/dot_general | solution.py:13
  240.8 6.9 %collective-permute-done = f32[8,2048]{1,0:T(8,128)S(1)} collective-permute-done((f32[8,2048]{1,0:T(8,128)S(1)}, f32[8,2048]{1,0:T(8,128)S(1)}, u32[]{:S(2)}, u32[]{:S(2)}) %collective-permute-start) | collective-permute-done | bytes 65568 | tf_op jit(solution)/shard_map/while/body/eval_jaxpr/ppermute | solution.py:9
  247.8 9.2 %convolution_dynamic-update-slice_fusion.3 = f32[64,1024]{1,0:T(8,128)S(1)} fusion(f32[64,1024]{1,0:T(8,128)S(1)} %get-tuple-element.191, s32[]{:T(128)S(6)} %select_n.41, f32[8,2048]{1,0:T(8,128)S(1)} %collective-permute-done, f32[1024,2048]{1,0:T(8,128)} %get-tuple-element.203), kind=kOutput, calls=%fused_computation.clone.1 | convolution fusion | flops 201326592 | bytes 8486916 | tf_op jit(solution)/shard_map/while/body/eval_jaxpr/dot_general | solution.py:13
  257.1 29.5 %psum.14 = f32[64]{0:T(128)S(1)} all-reduce(f32[64]{0:T(128)S(1)} %reduce_sum.18), channel_id=1, replica_groups=mesh['groups'=2,'blk'=8,'docs'=2] {'blk','docs'}, use_global_device_ids=true, to_apply=%region_4.5 | all-reduce | flops 64 | bytes 512 | tf_op jit(solution)/shard_map/psum | solution.py:56
  286.8 29.5 %psum.15 = f32[64]{0:T(128)S(1)} all-reduce(f32[64]{0:T(128)S(1)} %multiply_reduce_fusion), channel_id=1, replica_groups=mesh['groups'=2,'blk'=8,'docs'=2] {'blk','docs'}, use_global_device_ids=true, to_apply=%region_6.7 | all-reduce | flops 64 | bytes 512 | tf_op jit(solution)/shard_map/psum | solution.py:59
  (25 shorter events, 1.9 us)
Async XLA Ops:
  6.5 32.9 %copy-start = (bf16[128,2048]{1,0:T(8,128)(2,1)S(1)}, bf16[128,2048]{1,0:T(8,128)(2,1)}, u32[]{:S(2)}) copy-start(bf16[128,2048]{1,0:T(8,128)(2,1)} %param.6) | copy-start | bytes 1572868
  6.5 125.2 %all-reduce.3.cloned.1.call-start = ((), (), s32[]{:S(2)}) async-start(), calls=%async_computation | async-start | bytes 1048576
  143.8 7.1 %collective-permute-start = (f32[8,2048]{1,0:T(8,128)S(1)}, f32[8,2048]{1,0:T(8,128)S(1)}, u32[]{:S(2)}, u32[]{:S(2)}) collective-permute-start(f32[8,2048]{1,0:T(8,128)S(1)} %get-tuple-element.192), channel_id=1, source_target_pairs={{0,2},{2,4},{4,6},{6,8},{8,10},{10,12},{12,14},{14,0},{1,3},{3,5},... | collective-permute-start | bytes 196616 | tf_op jit(solution)/shard_map/while/body/eval_jaxpr/ppermute | solution.py:9
  160.0 7.0 %collective-permute-start = (f32[8,2048]{1,0:T(8,128)S(1)}, f32[8,2048]{1,0:T(8,128)S(1)}, u32[]{:S(2)}, u32[]{:S(2)}) collective-permute-start(f32[8,2048]{1,0:T(8,128)S(1)} %get-tuple-element.192), channel_id=1, source_target_pairs={{0,2},{2,4},{4,6},{6,8},{8,10},{10,12},{12,14},{14,0},{1,3},{3,5},... | collective-permute-start | bytes 196616 | tf_op jit(solution)/shard_map/while/body/eval_jaxpr/ppermute | solution.py:9
  176.2 7.0 %collective-permute-start = (f32[8,2048]{1,0:T(8,128)S(1)}, f32[8,2048]{1,0:T(8,128)S(1)}, u32[]{:S(2)}, u32[]{:S(2)}) collective-permute-start(f32[8,2048]{1,0:T(8,128)S(1)} %get-tuple-element.192), channel_id=1, source_target_pairs={{0,2},{2,4},{4,6},{6,8},{8,10},{10,12},{12,14},{14,0},{1,3},{3,5},... | collective-permute-start | bytes 196616 | tf_op jit(solution)/shard_map/while/body/eval_jaxpr/ppermute | solution.py:9
  192.3 7.0 %collective-permute-start = (f32[8,2048]{1,0:T(8,128)S(1)}, f32[8,2048]{1,0:T(8,128)S(1)}, u32[]{:S(2)}, u32[]{:S(2)}) collective-permute-start(f32[8,2048]{1,0:T(8,128)S(1)} %get-tuple-element.192), channel_id=1, source_target_pairs={{0,2},{2,4},{4,6},{6,8},{8,10},{10,12},{12,14},{14,0},{1,3},{3,5},... | collective-permute-start | bytes 196616 | tf_op jit(solution)/shard_map/while/body/eval_jaxpr/ppermute | solution.py:9
  208.5 7.0 %collective-permute-start = (f32[8,2048]{1,0:T(8,128)S(1)}, f32[8,2048]{1,0:T(8,128)S(1)}, u32[]{:S(2)}, u32[]{:S(2)}) collective-permute-start(f32[8,2048]{1,0:T(8,128)S(1)} %get-tuple-element.192), channel_id=1, source_target_pairs={{0,2},{2,4},{4,6},{6,8},{8,10},{10,12},{12,14},{14,0},{1,3},{3,5},... | collective-permute-start | bytes 196616 | tf_op jit(solution)/shard_map/while/body/eval_jaxpr/ppermute | solution.py:9
  224.7 7.0 %collective-permute-start = (f32[8,2048]{1,0:T(8,128)S(1)}, f32[8,2048]{1,0:T(8,128)S(1)}, u32[]{:S(2)}, u32[]{:S(2)}) collective-permute-start(f32[8,2048]{1,0:T(8,128)S(1)} %get-tuple-element.192), channel_id=1, source_target_pairs={{0,2},{2,4},{4,6},{6,8},{8,10},{10,12},{12,14},{14,0},{1,3},{3,5},... | collective-permute-start | bytes 196616 | tf_op jit(solution)/shard_map/while/body/eval_jaxpr/ppermute | solution.py:9
  240.8 7.0 %collective-permute-start = (f32[8,2048]{1,0:T(8,128)S(1)}, f32[8,2048]{1,0:T(8,128)S(1)}, u32[]{:S(2)}, u32[]{:S(2)}) collective-permute-start(f32[8,2048]{1,0:T(8,128)S(1)} %get-tuple-element.192), channel_id=1, source_target_pairs={{0,2},{2,4},{4,6},{6,8},{8,10},{10,12},{12,14},{14,0},{1,3},{3,5},... | collective-permute-start | bytes 196616 | tf_op jit(solution)/shard_map/while/body/eval_jaxpr/ppermute | solution.py:9
Sparse Core Ops, SparseCore 0:
  40.6 91.0 all-reduce.2
where the time goes:
time: 324 us
  waiting for transfers between devices  138 us (43%)
  blocking collectives  93.8 us (29%)
  matrix products  74.5 us (23%)
  between operations  14 us (4%)
    unnamed x2, waiting for transfers between devices  89.5 us
    dot_general x8, matrix products, block_scores(): lax.dot_general(block, documents, (((1,), (1,)), ((), ())), precision=lax...  73.4 us
    ppermute x7, waiting for transfers between devices, from_behind(): lax.ppermute(value, axis, [(i, (i + by) % length) for i in range(length)])  48.2 us
    all_gather x1, blocking collectives, per_device(): all_queries = lax.all_gather(queries, 'blk', axis=0, tiled=True)  32.9 us
    psum x1, blocking collectives, per_device(): total = lax.psum(jnp.sum(scores, axis=1), ('blk', 'docs'))  29.5 us
    psum x1, blocking collectives, per_device(): spread = lax.psum(jnp.sum(centered * centered, axis=1), ('blk', 'docs'))  29.5 us
  transfers between devices with their start and end apart: 8, of which 8 were waited for; matrix products, arithmetic and copies ran while one was open for 0% of the time, Pallas kernels for 0%

commit v1 on v0

--- a/solution.py
+++ b/solution.py
@@ -1,7 +1,15 @@
+import functools
 import jax
 import jax.numpy as jnp
 from jax import lax
+from jax.experimental import pallas as pl
+from jax.experimental.pallas import tpu as pltpu
 from jax.sharding import PartitionSpec as P
+
+F32 = jnp.float32
+BF16 = jnp.bfloat16
+MESH = pl.DeviceIdType.MESH
+NT = (((1,), (1,)), ((), ()))
 
 
 def from_behind(value, axis, by):
@@ -13,13 +21,13 @@
     return lax.dot_general(
         block,
         documents,
-        (((1,), (1,)), ((), ())),
+        NT,
         precision=lax.Precision.HIGHEST,
         preferred_element_type=jnp.float32,
     )
 
 
-def per_device(queries, whiten, documents):
+def ring_plan(queries, whiten, documents):
     q_rows = queries.shape[0]
     n_blk = lax.axis_size("blk")
     n_docs = lax.axis_size("docs")
@@ -51,7 +59,7 @@
         held = place(held, moving, (here - turn) % n_blk)
         return (held, moving)
 
-    scores, moving = lax.fori_loop(1, n_blk, step_one, (scores, whitened))
+    scores, _ = lax.fori_loop(1, n_blk, step_one, (scores, whitened))
     count = jnp.float32(documents.shape[0] * n_blk * n_docs)
     total = lax.psum(jnp.sum(scores, axis=1), ("blk", "docs"))
     mean = total / count
@@ -61,6 +69,322 @@
     return centered * lax.rsqrt(variance + 1e-05)[:, None]
 
 
+def flip(index, mask):
+    bit = 1
+    while bit <= mask:
+        if mask & bit:
+            index = index + bit - 2 * bit * ((index // bit) % 2)
+        bit *= 2
+    return index
+
+
+def split(value):
+    high = value.astype(BF16)
+    return high, (value - high.astype(F32)).astype(BF16)
+
+
+def kernel(
+    n_blk,
+    q_ref,
+    wh_ref,
+    d_ref,
+    out_ref,
+    qbuf,
+    whbuf,
+    pbuf,
+    rbuf,
+    ag,
+    dbuf,
+    dhi,
+    dlo,
+    stats,
+    loc_sem,
+    doc_sem,
+    q_send,
+    q_recv,
+    wh_send,
+    wh_recv,
+    r_send,
+    r_recv,
+    a_send,
+    a_recv,
+    f_send,
+    f_recv,
+    s_send,
+    s_recv,
+):
+    here = lax.axis_index("blk")
+    core = lax.axis_index("docs")
+    other = 1 - core
+    q_rows = q_ref.shape[0]
+    depth = qbuf.shape[2]
+    wide = pbuf.shape[2]
+    half = n_blk * wide
+    nq = n_blk * q_rows
+    docs = d_ref.shape[0]
+    slabs = doc_sem.shape[0]
+    slab = docs // slabs
+    peers = range(1, n_blk)
+    far_first = list(reversed(peers))
+
+    def remote(src, dst, send, recv, blk, docs_index):
+        return pltpu.make_async_remote_copy(
+            src_ref=src,
+            dst_ref=dst,
+            send_sem=send,
+            recv_sem=recv,
+            device_id={"blk": blk, "docs": docs_index},
+            device_id_type=MESH,
+        )
+
+    def cols(start, size):
+        return pl.ds(pl.multiple_of(start, 128), size)
+
+    own_q = pltpu.make_async_copy(
+        q_ref.at[:, cols(here * depth, depth)], qbuf.at[here], loc_sem.at[0]
+    )
+    own_wh = pltpu.make_async_copy(
+        wh_ref.at[:, cols(core * half, half)], whbuf.at[core], loc_sem.at[1]
+    )
+    own_q.start()
+    own_wh.start()
+    doc_copies = [
+        pltpu.make_async_copy(
+            d_ref.at[pl.ds(s * slab, slab)], dbuf.at[pl.ds(s * slab, slab)], doc_sem.at[s]
+        )
+        for s in range(slabs)
+    ]
+    for copy in doc_copies:
+        copy.start()
+
+    barrier = pltpu.get_barrier_semaphore()
+    for i in range(n_blk):
+        for c in (core, other):
+            if i == 0 and c is core:
+                continue
+            pl.semaphore_signal(
+                barrier,
+                inc=1,
+                device_id={"blk": flip(here, i), "docs": c},
+                device_id_type=MESH,
+            )
+    pl.semaphore_wait(barrier, 2 * n_blk - 1)
+
+    q_copies = {}
+    for i in far_first:
+        to = flip(here, i)
+        q_copies[i] = remote(
+            q_ref.at[:, cols(to * depth, depth)],
+            qbuf.at[here],
+            q_send.at[i],
+            q_recv.at[i],
+            to,
+            core,
+        )
+        q_copies[i].start()
+    wh_copy = remote(
+        wh_ref.at[:, cols(other * half, half)],
+        whbuf.at[core],
+        wh_send,
+        wh_recv,
+        here,
+        other,
+    )
+    wh_copy.start()
+
+    own_q.wait()
+    own_wh.wait()
+    wh_copy.wait_recv()
+    for i in peers:
+        q_copies[i].wait_recv()
+
+    query_cols = qbuf[...].astype(F32).reshape(nq, depth).astype(BF16)
+    rows = whbuf[...].reshape(depth, half)
+    partial = jnp.dot(query_cols, rows, preferred_element_type=F32)
+    for b in range(n_blk):
+        pbuf[b] = partial[:, b * wide : (b + 1) * wide]
+
+    r_copies = {}
+    for i in far_first:
+        to = flip(here, i)
+        r_copies[i] = remote(
+            pbuf.at[to], rbuf.at[i - 1], r_send.at[i], r_recv.at[i], to, core
+        )
+        r_copies[i].start()
+
+    step = 32
+    for s in range(slabs):
+        doc_copies[s].wait()
+
+        def one(t, carry):
+            at = pl.ds(pl.multiple_of(s * slab + t * step, step), step)
+            for b in range(n_blk):
+                for h in range(2):
+                    high, low = split(dbuf[at, pl.ds(h * half + b * wide, wide)])
+                    dhi[b, at, pl.ds(h * wide, wide)] = high
+                    dlo[b, at, pl.ds(h * wide, wide)] = low
+            return carry
+
+        lax.fori_loop(0, slab // step, one, 0)
+
+    own = pbuf[here]
+    for i in peers:
+        r_copies[i].wait_recv()
+        own = own + rbuf[i - 1]
+    high, low = split(own)
+    ag[core, 0, 0:nq] = high
+    ag[core, 0, nq : 2 * nq] = low
+
+    def across(i):
+        return remote(
+            ag.at[core, i], ag.at[core, i], f_send.at[i], f_recv.at[i], here, other
+        )
+
+    a_copies = {}
+    for i in far_first:
+        a_copies[i] = remote(
+            ag.at[core, 0], ag.at[core, i], a_send.at[i], a_recv.at[i], flip(here, i), core
+        )
+        a_copies[i].start()
+    f_copies = [across(0)]
+    f_copies[0].start()
+
+    for i in range(n_blk):
+        if i + 1 < n_blk:
+            a_copies[i + 1].wait_recv()
+            f_copies.append(across(i + 1))
+            f_copies[i + 1].start()
+        f_copies[i].wait_recv()
+        chunk = flip(here, i)
+        left = jnp.concatenate([ag[0, i], ag[1, i]], axis=1)
+        both = lax.dot_general(left, dhi[chunk], NT, preferred_element_type=F32)
+        term = both[:nq] + both[nq:]
+        term += lax.dot_general(left[:nq], dlo[chunk], NT, preferred_element_type=F32)
+        if i == 0:
+            out_ref[...] = term
+        else:
+            out_ref[...] += term
+
+    scores = out_ref[...]
+    lanes = stats.shape[2]
+    eye = lax.broadcasted_iota(jnp.int32, (nq, lanes), 0) == lax.broadcasted_iota(
+        jnp.int32, (nq, lanes), 1
+    )
+
+    def to_row(column):
+        return jnp.sum(jnp.where(eye, column, 0.0), axis=0, keepdims=True)
+
+    def to_column(row):
+        return jnp.sum(jnp.where(eye, row, 0.0), axis=1, keepdims=True)
+
+    local_mean = jnp.sum(scores, axis=1, keepdims=True) * (1.0 / docs)
+    centered = scores - local_mean
+    local_spread = jnp.sum(centered * centered, axis=1, keepdims=True)
+    mine = here * 2 + core
+    stats[mine, 0:1] = to_row(local_mean)
+    stats[mine, 1:2] = to_row(local_spread)
+    s_copies = []
+    for i in reversed(range(n_blk)):
+        for c in (core, other):
+            if i == 0 and c is core:
+                continue
+            k = 2 * i + (0 if c is core else 1)
+            copy = remote(
+                stats.at[mine],
+                stats.at[mine],
+                s_send.at[k],
+                s_recv.at[k],
+                flip(here, i),
+                c,
+            )
+            copy.start()
+            s_copies.append(copy)
+    for copy in s_copies:
+        copy.wait_recv()
+    means = stats[:, 0, :]
+    spreads = stats[:, 1, :]
+    n_dev = 2 * n_blk
+    mean = jnp.sum(means, axis=0, keepdims=True) * (1.0 / n_dev)
+    away = means - mean
+    spread = jnp.sum(spreads + docs * (away * away), axis=0, keepdims=True)
+    scale = lax.rsqrt(spread * (1.0 / (docs * n_dev)) + 1e-05)
+    out_ref[...] = (scores - to_column(mean)) * to_column(scale)
+
+    for i in peers:
+        q_copies[i].wait_send()
+        r_copies[i].wait_send()
+        a_copies[i].wait_send()
+    wh_copy.wait_send()
+    for copy in f_copies + s_copies:
+        copy.wait_send()
+
+
+def kernel_plan(queries, whiten, documents):
+    n_blk = lax.axis_size("blk")
+    q_rows, k = queries.shape
+    span = whiten.shape[0]
+    docs = documents.shape[0]
+    depth = 2 * span
+    half = k // 2
+    wide = half // n_blk
+    nq = q_rows * n_blk
+    slabs = 8
+    dma = pltpu.SemaphoreType.DMA
+    return pl.pallas_call(
+        functools.partial(kernel, n_blk),
+        out_shape=jax.ShapeDtypeStruct((nq, docs), F32),
+        in_specs=[pl.BlockSpec(memory_space=pl.ANY)] * 3,
+        out_specs=pl.BlockSpec(memory_space=pltpu.VMEM),
+        scratch_shapes=[
+            pltpu.VMEM((n_blk, q_rows, depth), BF16),
+            pltpu.VMEM((2, span, half), BF16),
+            pltpu.VMEM((n_blk, nq, wide), F32),
+            pltpu.VMEM((n_blk - 1, nq, wide), F32),
+            pltpu.VMEM((2, n_blk, 2 * nq, wide), BF16),
+            pltpu.VMEM((docs, k), F32),
+            pltpu.VMEM((n_blk, docs, 2 * wide), BF16),
+            pltpu.VMEM((n_blk, docs, 2 * wide), BF16),
+            pltpu.VMEM((2 * n_blk, 2, 128), F32),
+            dma((2,)),
+            dma((slabs,)),
+            dma((n_blk,)),
+            dma((n_blk,)),
+            dma,
+            dma,
+            dma((n_blk,)),
+            dma((n_blk,)),
+            dma((n_blk,)),
+            dma((n_blk,)),
+            dma((n_blk,)),
+            dma((n_blk,)),
+            dma((2 * n_blk,)),
+            dma((2 * n_blk,)),
+        ],
+        compiler_params=pltpu.CompilerParams(
+            collective_id=0, has_side_effects=True, vmem_limit_bytes=40 * 2**20
+        ),
+    )(queries, whiten, documents)
+
+
+def per_device(queries, whiten, documents):
+    n_blk = lax.axis_size("blk")
+    q_rows, k = queries.shape
+    fits = (
+        lax.axis_size("docs") == 2
+        and n_blk & (n_blk - 1) == 0
+        and n_blk * 2 * whiten.shape[0] == k
+        and whiten.shape[0] % 128 == 0
+        and k % (256 * n_blk) == 0
+        and q_rows % 8 == 0
+        and q_rows * n_blk <= 128
+        and documents.shape[0] % 256 == 0
+        and documents.shape[0] * k <= 2**21
+    )
+    if fits:
+        return kernel_plan(queries, whiten, documents)
+    return ring_plan(queries, whiten, documents)
+
+
 def solution(mesh):
     placed = (
         P(("groups", "blk"), None),

time: 324 us -> 38.3 us (0.12)
  waiting for transfers between devices: 138 us -> 0 us
  blocking collectives: 93.8 us -> 0 us
  matrix products: 74.5 us -> 0 us
  Pallas kernels: 0 us -> 32.1 us
  between operations: 14 us -> 0.01 us
  local copies, waits for them, and re-layouts: 2.17 us -> 5.88 us
    unnamed x2 -> x0, waiting for transfers between devices: 89.5 us -> none
    dot_general x9 -> x0, matrix products: 74.5 us -> none  [the longest x8 73.4 us: block_scores(): lax.dot_general(block, documents, (((1,), (1,)), ((), ())), precision=lax...]
    psum x2 -> x0, blocking collectives: 59 us -> none  [the longest x1 29.5 us: per_device(): total = lax.psum(jnp.sum(scores, axis=1), ('blk', 'docs'))]
    ppermute x7 -> x0, waiting for transfers between devices: 48.2 us -> none  [from_behind(): lax.ppermute(value, axis, [(i, (i + by) % length) for i in range(length)])]
    all_gather x2 -> x0, blocking collectives: 34.8 us -> none  [the longest x1 32.9 us: per_device(): all_queries = lax.all_gather(queries, 'blk', axis=0, tiled=True)]
    pallas_call x0 -> x1, Pallas kernels: none -> 32.1 us  [kernel_plan(): pl.pallas_call(functools.partial(kernel, n_blk), out_shape=jax.ShapeDtype...]
    unnamed x5 -> x7, local copies, waits for them, and re-layouts: 2.12 us -> 5.88 us
  transfers between devices with their start and end apart: 8 -> 0, of which waited for: 8 -> 0; matrix products, arithmetic and copies ran while one was open for 0% -> 0% of each run, Pallas kernels for 0% -> 0%
where the time goes in v1:
time: 38.3 us; the launch traced here: 38 us
  Pallas kernels  32.1 us (84%)
  local copies, waits for them, and re-layouts  5.88 us (15%)
    pallas_call x1, Pallas kernels, kernel_plan(): pl.pallas_call(functools.partial(kernel, n_blk), out_shape=jax.ShapeDtype...  32.1 us
    unnamed x7, local copies, waits for them, and re-layouts  5.88 us

profile of v1, /device:TPU:0, one launch (start us, length us, event | category | flops | bytes accessed | tf_op | source)
XLA Modules:
  0.0 38.0 jit_solution(6272472634606385957)
XLA Ops:
  0.0 0.0 copy-start
  0.0 3.4 %copy-done = f32[1024,2048]{1,0:T(8,128)S(1)} copy-done((f32[1024,2048]{1,0:T(8,128)S(1)}, f32[1024,2048]{1,0:T(8,128)}, u32[]{:S(2)}) %copy-start) | copy-done | bytes 8388632
  3.4 0.0 copy-start.1
  3.4 1.0 %copy-done.1 = bf16[128,2048]{1,0:T(8,128)(2,1)S(1)} copy-done((bf16[128,2048]{1,0:T(8,128)(2,1)S(1)}, bf16[128,2048]{1,0:T(8,128)(2,1)}, u32[]{:S(2)}) %copy-start.1) | copy-done | bytes 524312
  4.4 0.0 copy-start.2
  4.4 0.8 %copy-done.2 = bf16[8,2048]{1,0:T(8,128)(2,1)S(1)} copy-done((bf16[8,2048]{1,0:T(8,128)(2,1)S(1)}, bf16[8,2048]{1,0:T(8,128)(2,1)}, u32[]{:S(2)}) %copy-start.2) | copy-done | bytes 32792
  5.2 32.1 %shard_map.37 = f32[64,1024]{1,0:T(8,128)S(1)} custom-call(bf16[8,2048]{1,0:T(8,128)(2,1)S(1)} %copy-done.2, bf16[128,2048]{1,0:T(8,128)(2,1)S(1)} %copy-done.1, f32[1024,2048]{1,0:T(8,128)S(1)} %copy-done), custom_call_target="tpu_custom_call" | custom-call | tf_op jit(solution)/shard_map/pallas_call | solution.py:333
  37.3 0.7 %copy.5 = f32[64,1024]{1,0:T(8,128)} copy(f32[64,1024]{1,0:T(8,128)S(1)} %shard_map.37) | data formatting | bytes 524288
Async XLA Ops:
  0.0 3.4 %copy-start = (f32[1024,2048]{1,0:T(8,128)S(1)}, f32[1024,2048]{1,0:T(8,128)}, u32[]{:S(2)}) copy-start(f32[1024,2048]{1,0:T(8,128)} %d_ref.1) | copy-start | bytes 25165828
  3.4 1.0 %copy-start.1 = (bf16[128,2048]{1,0:T(8,128)(2,1)S(1)}, bf16[128,2048]{1,0:T(8,128)(2,1)}, u32[]{:S(2)}) copy-start(bf16[128,2048]{1,0:T(8,128)(2,1)} %wh_ref.1) | copy-start | bytes 1572868
  4.4 0.8 %copy-start.2 = (bf16[8,2048]{1,0:T(8,128)(2,1)S(1)}, bf16[8,2048]{1,0:T(8,128)(2,1)}, u32[]{:S(2)}) copy-start(bf16[8,2048]{1,0:T(8,128)(2,1)} %q_ref.1) | copy-start | bytes 98308

commit v2 on v1

--- a/solution.py
+++ b/solution.py
@@ -170,6 +170,7 @@
             )
     pl.semaphore_wait(barrier, 2 * n_blk - 1)
 
+    sends = []
     q_copies = {}
     for i in far_first:
         to = flip(here, i)
@@ -182,6 +183,7 @@
             core,
         )
         q_copies[i].start()
+        sends.append(q_copies[i])
     wh_copy = remote(
         wh_ref.at[:, cols(other * half, half)],
         whbuf.at[core],
@@ -191,6 +193,7 @@
         other,
     )
     wh_copy.start()
+    sends.append(wh_copy)
 
     own_q.wait()
     own_wh.wait()
@@ -211,6 +214,7 @@
             pbuf.at[to], rbuf.at[i - 1], r_send.at[i], r_recv.at[i], to, core
         )
         r_copies[i].start()
+        sends.append(r_copies[i])
 
     step = 32
     for s in range(slabs):
@@ -246,6 +250,7 @@
             ag.at[core, 0], ag.at[core, i], a_send.at[i], a_recv.at[i], flip(here, i), core
         )
         a_copies[i].start()
+        sends.append(a_copies[i])
     f_copies = [across(0)]
     f_copies[0].start()
 
@@ -310,12 +315,7 @@
     scale = lax.rsqrt(spread * (1.0 / (docs * n_dev)) + 1e-05)
     out_ref[...] = (scores - to_column(mean)) * to_column(scale)
 
-    for i in peers:
-        q_copies[i].wait_send()
-        r_copies[i].wait_send()
-        a_copies[i].wait_send()
-    wh_copy.wait_send()
-    for copy in f_copies + s_copies:
+    for copy in sends + f_copies + s_copies:
         copy.wait_send()
 
 
@@ -333,7 +333,7 @@
     return pl.pallas_call(
         functools.partial(kernel, n_blk),
         out_shape=jax.ShapeDtypeStruct((nq, docs), F32),
-        in_specs=[pl.BlockSpec(memory_space=pl.ANY)] * 3,
+        in_specs=[pl.BlockSpec(memory_space=pltpu.HBM)] * 3,
         out_specs=pl.BlockSpec(memory_space=pltpu.VMEM),
         scratch_shapes=[
             pltpu.VMEM((n_blk, q_rows, depth), BF16),
@@ -361,7 +361,7 @@
             dma((2 * n_blk,)),
         ],
         compiler_params=pltpu.CompilerParams(
-            collective_id=0, has_side_effects=True, vmem_limit_bytes=40 * 2**20
+            collective_id=0, has_side_effects=True, vmem_limit_bytes=64 * 2**20
         ),
     )(queries, whiten, documents)
 

time: 38.3 us -> 34.2 us (0.89)
  local copies, waits for them, and re-layouts: 5.88 us -> 1.67 us
    unnamed x7 -> x1, local copies, waits for them, and re-layouts: 5.88 us -> 1.67 us
where the time goes in v2:
time: 34.2 us; the launch traced here: 34.1 us
  Pallas kernels  32.4 us (95%)
  local copies, waits for them, and re-layouts  1.67 us (5%)
    pallas_call x1, Pallas kernels, kernel_plan(): pl.pallas_call(functools.partial(kernel, n_blk), out_shape=jax.ShapeDtype...  32.4 us
    unnamed x1, local copies, waits for them, and re-layouts  1.67 us

profile of v2, /device:TPU:0, one launch (start us, length us, event | category | flops | bytes accessed | tf_op | source)
XLA Modules:
  0.0 34.1 jit_solution(15955056435352340497)
XLA Ops:
  0.0 32.4 %shard_map.37 = f32[64,1024]{1,0:T(8,128)} custom-call(bf16[8,2048]{1,0:T(8,128)(2,1)} %q_ref.1, bf16[128,2048]{1,0:T(8,128)(2,1)} %wh_ref.1, f32[1024,2048]{1,0:T(8,128)} %d_ref.1), custom_call_target="tpu_custom_call" | custom-call | tf_op jit(solution)/shard_map/pallas_call | solution.py:333
  32.4 1.7 %copy.5 = f32[64,1024]{1,0:T(8,128)} copy(f32[64,1024]{1,0:T(8,128)} %shard_map.37) | data formatting | bytes 524288

commit v3 on v2

--- a/solution.py
+++ b/solution.py
@@ -97,6 +97,7 @@
     dbuf,
     dhi,
     dlo,
+    acc,
     stats,
     loc_sem,
     doc_sem,
@@ -154,11 +155,9 @@
         )
         for s in range(slabs)
     ]
-    for copy in doc_copies:
-        copy.start()
 
     barrier = pltpu.get_barrier_semaphore()
-    for i in range(n_blk):
+    for i in reversed(range(n_blk)):
         for c in (core, other):
             if i == 0 and c is core:
                 continue
@@ -195,6 +194,9 @@
     wh_copy.start()
     sends.append(wh_copy)
 
+    for copy in doc_copies:
+        copy.start()
+
     own_q.wait()
     own_wh.wait()
     wh_copy.wait_recv()
@@ -207,14 +209,16 @@
     for b in range(n_blk):
         pbuf[b] = partial[:, b * wide : (b + 1) * wide]
 
+    def reduce_copy(i, src, to):
+        copy = remote(src, rbuf.at[i - 1], r_send.at[i], r_recv.at[i], to, core)
+        copy.start()
+        sends.append(copy)
+        return copy
+
     r_copies = {}
-    for i in far_first:
+    for i in (7, 6, 5, 4, 3, 2, 1):
         to = flip(here, i)
-        r_copies[i] = remote(
-            pbuf.at[to], rbuf.at[i - 1], r_send.at[i], r_recv.at[i], to, core
-        )
-        r_copies[i].start()
-        sends.append(r_copies[i])
+        r_copies[i] = reduce_copy(i, pbuf.at[to], to)
 
     step = 32
     for s in range(slabs):
@@ -244,33 +248,37 @@
             ag.at[core, i], ag.at[core, i], f_send.at[i], f_recv.at[i], here, other
         )
 
-    a_copies = {}
-    for i in far_first:
-        a_copies[i] = remote(
-            ag.at[core, 0], ag.at[core, i], a_send.at[i], a_recv.at[i], flip(here, i), core
-        )
-        a_copies[i].start()
-        sends.append(a_copies[i])
-    f_copies = [across(0)]
+    def gather_copy(i, src, to):
+        copy = remote(ag.at[core, src], ag.at[core, i], a_send.at[i], a_recv.at[i], to, core)
+        copy.start()
+        sends.append(copy)
+        return copy
+
+    a_copies = {i: gather_copy(i, 0, flip(here, i)) for i in (4, 7, 6, 3, 2, 1)}
+    f_copies = {0: across(0)}
     f_copies[0].start()
 
-    for i in range(n_blk):
-        if i + 1 < n_blk:
-            a_copies[i + 1].wait_recv()
-            f_copies.append(across(i + 1))
-            f_copies[i + 1].start()
+    order = (0, 1, 2, 4, 3, 6, 7, 5)
+    for n, i in enumerate(order):
+        if n + 1 < n_blk:
+            after = order[n + 1]
+            a_copies[after].wait_recv()
+            if after == 4:
+                a_copies[5] = gather_copy(5, 4, flip(here, 1))
+            f_copies[after] = across(after)
+            f_copies[after].start()
         f_copies[i].wait_recv()
         chunk = flip(here, i)
         left = jnp.concatenate([ag[0, i], ag[1, i]], axis=1)
         both = lax.dot_general(left, dhi[chunk], NT, preferred_element_type=F32)
         term = both[:nq] + both[nq:]
         term += lax.dot_general(left[:nq], dlo[chunk], NT, preferred_element_type=F32)
-        if i == 0:
-            out_ref[...] = term
+        if n == 0:
+            acc[...] = term
         else:
-            out_ref[...] += term
-
-    scores = out_ref[...]
+            acc[...] += term
+
+    scores = acc[...]
     lanes = stats.shape[2]
     eye = lax.broadcasted_iota(jnp.int32, (nq, lanes), 0) == lax.broadcasted_iota(
         jnp.int32, (nq, lanes), 1
@@ -315,7 +323,7 @@
     scale = lax.rsqrt(spread * (1.0 / (docs * n_dev)) + 1e-05)
     out_ref[...] = (scores - to_column(mean)) * to_column(scale)
 
-    for copy in sends + f_copies + s_copies:
+    for copy in sends + list(f_copies.values()) + s_copies:
         copy.wait_send()
 
 
@@ -330,7 +338,7 @@
     nq = q_rows * n_blk
     slabs = 8
     dma = pltpu.SemaphoreType.DMA
-    return pl.pallas_call(
+    scores = pl.pallas_call(
         functools.partial(kernel, n_blk),
         out_shape=jax.ShapeDtypeStruct((nq, docs), F32),
         in_specs=[pl.BlockSpec(memory_space=pltpu.HBM)] * 3,
@@ -344,6 +352,7 @@
             pltpu.VMEM((docs, k), F32),
             pltpu.VMEM((n_blk, docs, 2 * wide), BF16),
             pltpu.VMEM((n_blk, docs, 2 * wide), BF16),
+            pltpu.VMEM((nq, docs), F32),
             pltpu.VMEM((2 * n_blk, 2, 128), F32),
             dma((2,)),
             dma((slabs,)),
@@ -364,6 +373,7 @@
             collective_id=0, has_side_effects=True, vmem_limit_bytes=64 * 2**20
         ),
     )(queries, whiten, documents)
+    return scores
 
 
 def per_device(queries, whiten, documents):
@@ -371,7 +381,7 @@
     q_rows, k = queries.shape
     fits = (
         lax.axis_size("docs") == 2
-        and n_blk & (n_blk - 1) == 0
+        and n_blk == 8
         and n_blk * 2 * whiten.shape[0] == k
         and whiten.shape[0] % 128 == 0
         and k % (256 * n_blk) == 0

time: 34.2 us -> 33.5 us (0.980)
  Pallas kernels: 32.4 us -> 31.7 us
    pallas_call x1, Pallas kernels: 32.4 us -> 31.7 us  [kernel_plan(): pl.pallas_call(functools.partial(kernel, n_blk), out_shape=jax.ShapeDtype...]
where the time goes in v3:
time: 33.5 us; the launch traced here: 33.4 us
  Pallas kernels  31.7 us (95%)
  local copies, waits for them, and re-layouts  1.67 us (5%)
    pallas_call x1, Pallas kernels, kernel_plan(): pl.pallas_call(functools.partial(kernel, n_blk), out_shape=jax.ShapeDtype...  31.7 us
    unnamed x1, local copies, waits for them, and re-layouts  1.67 us

profile of v3, /device:TPU:0, one launch (start us, length us, event | category | flops | bytes accessed | tf_op | source)
XLA Modules:
  0.0 33.4 jit_solution(11858017061915102060)
XLA Ops:
  0.0 31.7 %shard_map.37 = f32[64,1024]{1,0:T(8,128)} custom-call(bf16[8,2048]{1,0:T(8,128)(2,1)} %q_ref.1, bf16[128,2048]{1,0:T(8,128)(2,1)} %wh_ref.1, f32[1024,2048]{1,0:T(8,128)} %d_ref.1), custom_call_target="tpu_custom_call" | custom-call | tf_op jit(solution)/shard_map/pallas_call | solution.py:341
  31.7 1.7 %copy.5 = f32[64,1024]{1,0:T(8,128)} copy(f32[64,1024]{1,0:T(8,128)} %shard_map.37) | data formatting | bytes 524288

commit v4 on v3

--- a/solution.py
+++ b/solution.py
@@ -258,7 +258,7 @@
     f_copies = {0: across(0)}
     f_copies[0].start()
 
-    order = (0, 1, 2, 4, 3, 6, 7, 5)
+    order = (0, 1, 4, 2, 3, 6, 7, 5)
     for n, i in enumerate(order):
         if n + 1 < n_blk:
             after = order[n + 1]

time: 33.5 us -> 33.1 us (0.988)
  Pallas kernels: 31.7 us -> 31.3 us
    pallas_call x1, Pallas kernels: 31.7 us -> 31.3 us  [kernel_plan(): pl.pallas_call(functools.partial(kernel, n_blk), out_shape=jax.ShapeDtype...]
where the time goes in v4:
time: 33.1 us; the launch traced here: 33 us
  Pallas kernels  31.3 us (95%)
  local copies, waits for them, and re-layouts  1.67 us (5%)
    pallas_call x1, Pallas kernels, kernel_plan(): pl.pallas_call(functools.partial(kernel, n_blk), out_shape=jax.ShapeDtype...  31.3 us
    unnamed x1, local copies, waits for them, and re-layouts  1.67 us

profile of v4, /device:TPU:0, one launch (start us, length us, event | category | flops | bytes accessed | tf_op | source)
XLA Modules:
  0.0 33.0 jit_solution(18008172387915536459)
XLA Ops:
  0.0 31.3 %shard_map.37 = f32[64,1024]{1,0:T(8,128)} custom-call(bf16[8,2048]{1,0:T(8,128)(2,1)} %q_ref.1, bf16[128,2048]{1,0:T(8,128)(2,1)} %wh_ref.1, f32[1024,2048]{1,0:T(8,128)} %d_ref.1), custom_call_target="tpu_custom_call" | custom-call | tf_op jit(solution)/shard_map/pallas_call | solution.py:341
  31.3 1.7 %copy.5 = f32[64,1024]{1,0:T(8,128)} copy(f32[64,1024]{1,0:T(8,128)} %shard_map.37) | data formatting | bytes 524288
